TPU v7x, 512 devices: a whole 4x8x8 slice. The times are simulated.
512 devices in a mesh: row: 16 (over y, core), col: 32 (over z, x).
Axes of the slice: x: 4, y: 8, z: 8, core: 2. Of those that a mesh axis runs over, the one named last changes fastest.
Arguments:
- old_vectors: float32 [8192, 4096], P('row', 'col'), may hold values from -6 to 6, as said below
- pole_values: float32 [8192], replicated, may hold values from 0 to 8192, as said below
- live_mask: int32 [8192], replicated, may hold values from 0 to 1, as said below
- position: int32 [8192], replicated, may hold values from 0 to 8191, as said below
- rank_weight: float32 [1], replicated, may hold values from 0.5 to 2
Outputs:
- new_vectors: float32 [8192, 8192], P('row', 'col')
Inputs may be any that keep to these rules, and one draw needn't show every extreme that they name: `pole_values`: strictly increasing; consecutive values differ by 0.2 or more. `old_vectors`: the entries of rows 4095 and 4096 have magnitude 0.5 to 1.5. Each merged position appears exactly once. In every aligned group of 16 consecutive columns s of the halves' eigenvectors (s = h * 4096 + m), exactly 12 have live_mask[position[s]] = 1.
All inputs are finite; a program needn't handle non-finite values.
Results may differ from a plain program's by a relative error of at most 0.0003.
Values sent between devices are 32-bit elements; how exact they have to be, the bound alone decides.
A program may use at most 64 MiB of HBM per device.

v0:
```python
import jax
import jax.numpy as jnp
from jax import lax
from jax.sharding import PartitionSpec as P

BISECT = 40


def bracket_lengths(pole_values, live_mask, squares, rank_value):
    order_size = pole_values.shape[0]
    positions = jnp.arange(order_size, dtype=jnp.int32)
    marked = jnp.where(live_mask > 0, positions, order_size)
    shifted = jnp.concatenate([marked[1:], jnp.full((1,), order_size, jnp.int32)])
    following = lax.cummin(shifted, axis=0, reverse=True)
    weight_sum = rank_value * jnp.sum(squares)
    next_gap = pole_values[jnp.minimum(following, order_size - 1)] - pole_values
    return jnp.where(following < order_size, next_gap, weight_sum)


def bisect_roots(pole_here, bracket_len, pole_values, squares, live_mask, rank_value):
    pole_diff = pole_values[None, :] - pole_here[:, None]
    alive_cols = (live_mask > 0)[None, :]

    def halving(interval, unused):
        low_end, high_end = interval
        middle = 0.5 * (low_end + high_end)
        offset_gap = pole_diff - middle[:, None]
        summands = jnp.where(
            alive_cols, squares[None, :] / jnp.where(alive_cols, offset_gap, 1.0), 0.0
        )
        secular = 1.0 + rank_value * jnp.sum(summands, axis=1)
        is_below = secular < 0.0
        return ((jnp.where(is_below, middle, low_end), jnp.where(is_below, high_end, middle)), None)

    interval, unused = lax.scan(
        halving, (jnp.zeros_like(bracket_len), bracket_len), None, length=BISECT
    )
    return 0.5 * (interval[0] + interval[1])


def log_terms(pole_here, offsets, live_here, own_index, pole_values, live_mask):
    order_size = pole_values.shape[0]
    pole_diff = pole_values[None, :] - pole_here[:, None]
    on_pole = own_index[:, None] == jnp.arange(order_size, dtype=jnp.int32)[None, :]
    quotient = jnp.where(
        on_pole, offsets[:, None], 1.0 - offsets[:, None] / jnp.where(on_pole, 1.0, pole_diff)
    )
    in_play = (live_here[:, None] > 0) & (live_mask[None, :] > 0)
    logs = jnp.where(in_play, jnp.log(jnp.abs(jnp.where(in_play, quotient, 1.0))), 0.0)
    return jnp.sum(logs, axis=0)


def column_norms(pole_here, offsets, live_here, pole_values, live_mask, hat_weights):
    alive_cols = (live_mask > 0)[None, :]
    offset_gap = pole_values[None, :] - pole_here[:, None] - offsets[:, None]
    summands = jnp.where(
        alive_cols, hat_weights[None, :] ** 2 / jnp.where(alive_cols, offset_gap, 1.0) ** 2, 0.0
    )
    return jnp.where(live_here > 0, jnp.sqrt(jnp.sum(summands, axis=1)), 1.0)


def cauchy_tile(
    sorted_rows,
    pole_cols,
    offset_cols,
    norm_cols,
    live_cols,
    col_index,
    pole_values,
    live_mask,
    hat_weights,
):
    row_poles = pole_values[sorted_rows]
    row_hats = hat_weights[sorted_rows]
    row_live = live_mask[sorted_rows] > 0
    col_live = (live_cols > 0)[None, :]
    both_live = row_live[:, None] & col_live
    offset_gap = row_poles[:, None] - pole_cols[None, :] - offset_cols[None, :]
    entries = row_hats[:, None] / jnp.where(both_live, offset_gap, 1.0) / norm_cols[None, :]
    identity = (sorted_rows[:, None] == col_index[None, :]).astype(jnp.float32)
    return jnp.where(col_live, jnp.where(both_live, entries, 0.0), identity)


def hat_from(log_sum, coupling, live_mask, rank_value):
    return jnp.where(
        live_mask > 0, jnp.sign(coupling) * jnp.exp(0.5 * (log_sum - jnp.log(rank_value))), 0.0
    )


def shards(old_vectors, pole_values, live_mask, position, rank_weight):
    rank_value = rank_weight[0]
    order_size = pole_values.shape[0]
    half_order = order_size // 2
    rows_here = old_vectors.shape[0]
    row_count = lax.axis_size("row")
    col_count = lax.axis_size("col")
    row_rank = lax.axis_index("row")
    col_rank = lax.axis_index("col")
    upper_owner = (half_order - 1) // rows_here
    lower_owner = half_order // rows_here
    edge_rows = jnp.stack(
        [
            jnp.where(row_rank == upper_owner, old_vectors[(half_order - 1) % rows_here], 0.0),
            jnp.where(row_rank == lower_owner, old_vectors[half_order % rows_here], 0.0),
        ]
    )
    edge_rows = lax.psum(edge_rows, "row")
    edge_rows = lax.all_gather(edge_rows, "col", axis=1, tiled=True)
    boundary = jnp.concatenate([edge_rows[0], edge_rows[1]])
    spread = jnp.zeros((order_size,), jnp.float32).at[position].set(boundary)
    coupling = jnp.where(live_mask > 0, spread, 0.0)
    squares = coupling * coupling
    bracket_len = bracket_lengths(pole_values, live_mask, squares, rank_value)
    block_cols = order_size // col_count
    per_device = block_cols // row_count
    block_first = col_rank * block_cols
    own_first = block_first + row_rank * per_device
    block_index = block_first + jnp.arange(block_cols, dtype=jnp.int32)
    own_poles = lax.dynamic_slice_in_dim(pole_values, own_first, per_device)
    own_live = lax.dynamic_slice_in_dim(live_mask, own_first, per_device)
    own_bracket = lax.dynamic_slice_in_dim(bracket_len, own_first, per_device)
    block_poles = lax.dynamic_slice_in_dim(pole_values, block_first, block_cols)
    block_live = lax.dynamic_slice_in_dim(live_mask, block_first, block_cols)
    bisected = bisect_roots(own_poles, own_bracket, pole_values, squares, live_mask, rank_value)
    own_offsets = jnp.where(own_live > 0, bisected, 0.5 * own_bracket)
    block_offsets = lax.all_gather(own_offsets, "row", axis=0, tiled=True)
    grouped = (
        block_poles.reshape(row_count, per_device),
        block_offsets.reshape(row_count, per_device),
        block_live.reshape(row_count, per_device),
        block_index.reshape(row_count, per_device),
    )

    def log_group(members):
        return log_terms(members[0], members[1], members[2], members[3], pole_values, live_mask)

    partial_logs = jnp.sum(lax.map(log_group, grouped), axis=0)
    log_sum = lax.psum(partial_logs, "col")
    hat_weights = hat_from(log_sum, coupling, live_mask, rank_value)

    def norm_group(members):
        return column_norms(members[0], members[1], members[2], pole_values, live_mask, hat_weights)

    block_norms = lax.map(norm_group, (grouped[0], grouped[1], grouped[2])).reshape(block_cols)
    half_id = row_rank * rows_here // half_order
    half_base = half_id * half_order
    panel_piece = lax.all_gather(old_vectors, "col", axis=1, tiled=True)
    sorted_rows = lax.dynamic_slice_in_dim(position, half_base, panel_piece.shape[1])
    cauchy = cauchy_tile(
        sorted_rows,
        block_poles,
        block_offsets,
        block_norms,
        block_live,
        block_index,
        pole_values,
        live_mask,
        hat_weights,
    )
    return jnp.dot(
        panel_piece, cauchy, precision=lax.Precision.HIGHEST, preferred_element_type=jnp.float32
    )


def solution(mesh):
    in_specs = (P("row", "col"), P(), P(), P(), P())
    out_specs = P("row", "col")
    return jax.shard_map(shards, mesh=mesh, in_specs=in_specs, out_specs=out_specs, check_vma=False)
```

profile of v0, /device:TPU:32, one launch (start us, length us, event | category | flops | bytes accessed | tf_op | source)
XLA Modules:
  0.0 492.8 jit_solution(11255109670068731941)
XLA Ops:
  6.5 0.7 all-gather.2.cloned.1.call-update
  7.3 0.7 broadcast_select_fusion.2
  8.0 23.6 %psum.14 = f32[2,128]{1,0:T(2,128)S(1)} all-reduce(f32[2,128]{1,0:T(2,128)S(1)} %pad_maximum_fusion.1), channel_id=1, replica_groups=mesh['row'=16,'col'=32] {'row'}, use_global_device_ids=true, to_apply=%region_0.1 | all-reduce | flops 256 | bytes 2048 | tf_op jit(solution)/shard_map/psum | solution.py:107
  31.5 49.0 %all_gather.9 = f32[2,4096]{1,0:T(2,128)S(1)} all-gather(f32[2,128]{1,0:T(2,128)S(1)} %psum.14), channel_id=1, replica_groups=mesh['row'=16,'col'=32] {'col'}, dimensions={1}, use_global_device_ids=true | all-gather | bytes 33792 | tf_op jit(solution)/shard_map/all_gather | solution.py:108
  80.6 0.8 compare_select_fusion.4
  81.4 30.5 %scatter_custom_fusion = f32[8192]{0:T(1024)S(1)} fusion(s32[8192]{0:T(1024)S(1)} %compare_select_fusion.4, f32[8192]{0:T(1024)S(1)} %pad_maximum_fusion, f32[]{:T(128)} %constant.114.clone.1), kind=kCustom, calls=%fused_computation.74 | custom fusion | bytes 32772 | tf_op jit(solution)/shard_map/scatter | solution.py:110
  111.9 1.4 fusion.44
  113.4 2.3 reduce-window.9
  116.8 0.8 broadcast_compare_fusion.4
  117.5 0.8 dynamic_slice.52
  118.3 45.5 %gather_fusion.1 = f32[8192]{0:T(1024)S(1)} fusion(f32[8192]{0:T(1024)S(1)} %copy-done, s32[8192]{0:T(1024)S(1)} %broadcast_clamp_fusion), kind=kCustom, calls=%fused_computation.1 | custom fusion | bytes 98304 | tf_op jit(solution)/shard_map/gather | solution.py:16
  165.1 46.3 %while.37 = (s32[]{:T(128)}, f32[16]{0:T(128)S(1)}, f32[16]{0:T(128)S(1)}, f32[]{:T(128)}, pred[1,8192]{1,0:T(4,128)(4,1)S(1)}, /*index=5*/f32[8192]{0:T(1024)S(...) while((s32[]{:T(128)}, f32[16]{0:T(128)S(1)}, ...), condition=%wide.region_7.8_spmd.clone, body=%wide.region_5.7_spmd.clone.sunk | while | flops 786563 | bytes 91005 | solution.py:35
  169.1 0.7 compare_select_fusion.10
  191.1 0.7 compare_select_fusion.10
  211.5 1.3 dynamic-slice
  213.6 23.5 %all-reduce = f32[256]{0:T(256)S(1)} all-reduce(f32[256]{0:T(256)S(1)} %fusion.40), channel_id=1, replica_groups=mesh['row'=16,'col'=32] {'row'}, use_global_device_ids=true, to_apply=%add | all-reduce | flops 256 | bytes 2048
  237.4 10.5 %while.35 = (s32[]{:T(128)}, f32[16,8192]{1,0:T(8,128)S(1)}, s32[16,16]{1,0:T(8,128)S(1)}, s32[8192]{0:T(1024)S(1)}, s32[16,16]{1,0:T(8,128)S(1)}, /*index=5*/f3...) while((s32[]{:T(128)}, f32[16,8192]{1,0:T(8,128)S(1)}, ...), condition=%wide.region_10.11_spmd, body=%wide.region_8.10_spmd.sunk | while | flops 1441810 | bytes 181013 | solution.py:137
  247.9 23.0 %gather_fusion = s32[4096]{0:T(1024)S(1)} fusion(s32[8192]{0:T(1024)S(1)} %get-tuple-element.538, s32[4096]{0:T(1024)S(1)} %get-tuple-element.264), kind=kCustom, calls=%fused_computation | custom fusion | bytes 49152 | tf_op jit(solution)/shard_map/gather | solution.py:75
  270.9 23.0 %gather_fusion.3 = f32[4096]{0:T(1024)S(1)} fusion(f32[8192]{0:T(1024)S(1)} %get-tuple-element.537, s32[4096]{0:T(1024)S(1)} %get-tuple-element.264), kind=kCustom, calls=%fused_computation.3 | custom fusion | bytes 49152 | tf_op jit(solution)/shard_map/gather | solution.py:73
  294.1 140.3 %psum.15 = f32[8192]{0:T(1024)S(1)} all-reduce(f32[8192]{0:T(1024)S(1)} %reduce_sum.48), channel_id=1, replica_groups=mesh['row'=16,'col'=32] {'col'}, use_global_device_ids=true, to_apply=%region_12.13 | all-reduce | flops 8192 | bytes 65536 | tf_op jit(solution)/shard_map/psum | solution.py:138
  434.5 23.0 %gather_fusion.2 = f32[4096]{0:T(1024)S(1)} fusion(f32[8192]{0:T(1024)S(1)} %get-tuple-element.267, s32[4096]{0:T(1024)S(1)} %get-tuple-element.264), kind=kCustom, calls=%fused_computation.2 | custom fusion | bytes 49152 | tf_op jit(solution)/shard_map/gather | solution.py:74
  457.5 8.1 %while.36 = (s32[]{:T(128)}, f32[16,16]{1,0:T(8,128)S(1)}, s32[16,16]{1,0:T(8,128)S(1)}, s32[8192]{0:T(1024)S(1)}, f32[1,8192]{1,0:T(1,128)S(1)}, /*index=5*/f32...) while((s32[]{:T(128)}, f32[16,16]{1,0:T(8,128)S(1)}, ...), condition=%wide.region_15.16_spmd, body=%wide.region_13.15_spmd.sunk | while | flops 925714 | bytes 115569 | solution.py:144
  465.7 19.3 %fusion.34 = f32[512,256]{0,1:T(8,128)S(1)} fusion(f32[512,4096]{1,0:T(8,128)} %all-gather.2.cloned.1.call-done, s32[256]{0:T(256)S(1)} %iota_add_fusion, f32[256]{0:T(256)S(1)} %div.58, f32[256]{0:T(256)S(1)} %all-reduce, f32[256]{0:T(256)S(1)} %dynamic_slice.52, f32[4096]{0:T(1024)S(1)} %gather_fusion.3, f32[4096]{0:T(1024)S(1)} %gather_fusion.2, ...), kind=kOutput, calls=%fused_computation.60 | convolution fusion | flops 6452936704 | bytes 8970496 | tf_op jit(solution)/shard_map/dot_general | solution.py:160
  485.0 1.0 copy.8
  (371 shorter events, 62.7 us)
Async XLA Ops:
  6.5 111.8 %copy-start = (f32[8192]{0:T(1024)S(1)}, f32[8192]{0:T(1024)}, u32[]{:S(2)}) copy-start(f32[8192]{0:T(1024)} %param.12) | copy-start | bytes 98308
  6.5 459.1 %all-gather.2.cloned.1.call-start = ((), (), s32[]{:S(2)}) async-start(), calls=%async_computation | async-start | bytes 8650752 | tf_op jit(solution)/shard_map/all_gather | solution.py:147
  118.3 95.1 %copy-start.1 = (s32[8192]{0:T(1024)S(1)}, s32[8192]{0:T(1024)}, u32[]{:S(2)}) copy-start(s32[8192]{0:T(1024)} %param.13) | copy-start | bytes 98308
  118.3 129.6 %copy-start.2 = (s32[8192]{0:T(1024)S(1)}, s32[8192]{0:T(1024)}, u32[]{:S(2)}) copy-start(s32[8192]{0:T(1024)} %param.14) | copy-start | bytes 98308
Sparse Core Ops, SparseCore 0:
  10.4 114.0 all-gather.1
where the time goes:
time: 494 us; the launch traced here: 493 us
  blocking collectives  236 us (48%)
  local copies, waits for them, and re-layouts  152 us (31%)
  other arithmetic  65.8 us (13%)
  matrix products  19.3 us (4%)
  between operations  15.6 us (3%)
    psum x1, blocking collectives, shards(): log_sum = lax.psum(partial_logs, 'col')  140 us
    all_gather x1, blocking collectives, shards(): edge_rows = lax.all_gather(edge_rows, 'col', axis=1, tiled=True)  49 us
    gather x1, local copies, waits for them, and re-layouts, bracket_lengths(): next_gap = pole_values[jnp.minimum(following, order_size - 1)] - pole_values  45.5 us
    scatter x1, local copies, waits for them, and re-layouts, shards(): spread = jnp.zeros((order_size,), jnp.float32).at[position].set(boundary)  30.5 us
    select_n x40, other arithmetic, halving(): jnp.where(is_below, high_end, middle)  26.3 us
    psum x1, blocking collectives, shards(): edge_rows = lax.psum(edge_rows, 'row')  23.6 us
    unnamed x1, blocking collectives  23.5 us
    gather x1, local copies, waits for them, and re-layouts, cauchy_tile(): row_live = live_mask[sorted_rows] > 0  23 us
  transfers between devices with their start and end apart: 1, of which 0 were waited for; matrix products, arithmetic and copies ran while one was open for 44% of the time, Pallas kernels for 0%

commit v1 on v0

--- a/solution.py
+++ b/solution.py
@@ -135,7 +135,7 @@
         return log_terms(members[0], members[1], members[2], members[3], pole_values, live_mask)
 
     partial_logs = jnp.sum(lax.map(log_group, grouped), axis=0)
-    log_sum = lax.psum(partial_logs, "col")
+    log_sum = jnp.sum(lax.all_gather(partial_logs, "col"), axis=0)
     hat_weights = hat_from(log_sum, coupling, live_mask, rank_value)
 
     def norm_group(members):

time: 494 us -> 465 us (0.941)
  the two profiles are of different devices: /device:TPU:32 before, /device:TPU:8 now
where the time goes in v1:
time: 465 us; the launch traced here: 464 us
  local copies, waits for them, and re-layouts  154 us (33%)
  waiting for transfers between devices  110 us (24%)
  blocking collectives  95.9 us (21%)
  other arithmetic  66.5 us (14%)
  matrix products  19.3 us (4%)
  between operations  15.6 us (3%)
    all_gather x1, waiting for transfers between devices, shards(): panel_piece = lax.all_gather(old_vectors, 'col', axis=1, tiled=True)  77.3 us
    all_gather x1, blocking collectives, shards(): edge_rows = lax.all_gather(edge_rows, 'col', axis=1, tiled=True)  46.5 us
    gather x1, local copies, waits for them, and re-layouts, bracket_lengths(): next_gap = pole_values[jnp.minimum(following, order_size - 1)] - pole_values  45.5 us
    all_gather x1, waiting for transfers between devices, shards(): log_sum = jnp.sum(lax.all_gather(partial_logs, 'col'), axis=0)  32 us
    scatter x1, local copies, waits for them, and re-layouts, shards(): spread = jnp.zeros((order_size,), jnp.float32).at[position].set(boundary)  30.5 us
    select_n x40, other arithmetic, halving(): jnp.where(is_below, high_end, middle)  26.3 us
    psum x1, blocking collectives, shards(): edge_rows = lax.psum(edge_rows, 'row')  25.9 us
    unnamed x1, blocking collectives  23.5 us
  transfers between devices with their start and end apart: 2, of which 2 were waited for; matrix products, arithmetic and copies ran while one was open for 17% of the time, Pallas kernels for 0%

profile of v1, /device:TPU:8, one launch (start us, length us, event | category | flops | bytes accessed | tf_op | source)
XLA Modules:
  0.0 463.8 jit_solution(6332349623287540392)
XLA Ops:
  6.5 0.7 broadcast_select_fusion.2
  7.3 25.9 %psum.7 = f32[2,128]{1,0:T(2,128)S(1)} all-reduce(f32[2,128]{1,0:T(2,128)S(1)} %pad_maximum_fusion.1), channel_id=1, replica_groups=mesh['row'=16,'col'=32] {'row'}, use_global_device_ids=true, to_apply=%region_0.1 | all-reduce | flops 256 | bytes 2048 | tf_op jit(solution)/shard_map/psum | solution.py:107
  33.2 46.5 %all_gather.15 = f32[2,4096]{1,0:T(2,128)S(1)} all-gather(f32[2,128]{1,0:T(2,128)S(1)} %psum.7), channel_id=1, replica_groups=mesh['row'=16,'col'=32] {'col'}, dimensions={1}, use_global_device_ids=true | all-gather | bytes 33792 | tf_op jit(solution)/shard_map/all_gather | solution.py:108
  79.7 0.8 compare_select_fusion.4
  80.5 30.5 %scatter_custom_fusion = f32[8192]{0:T(1024)S(1)} fusion(s32[8192]{0:T(1024)S(1)} %compare_select_fusion.4, f32[8192]{0:T(1024)S(1)} %pad_maximum_fusion, f32[]{:T(128)} %constant.114.clone.1), kind=kCustom, calls=%fused_computation.74 | custom fusion | bytes 32772 | tf_op jit(solution)/shard_map/scatter | solution.py:110
  110.9 1.4 fusion.44
  112.5 2.3 reduce-window.9
  115.8 0.8 broadcast_compare_fusion.4
  116.6 0.8 dynamic_slice.52
  117.3 45.5 %gather_fusion.1 = f32[8192]{0:T(1024)S(1)} fusion(f32[8192]{0:T(1024)S(1)} %copy-done, s32[8192]{0:T(1024)S(1)} %broadcast_clamp_fusion), kind=kCustom, calls=%fused_computation.1 | custom fusion | bytes 98304 | tf_op jit(solution)/shard_map/gather | solution.py:16
  164.2 46.3 %while.37 = (s32[]{:T(128)}, f32[16]{0:T(128)S(1)}, f32[16]{0:T(128)S(1)}, f32[]{:T(128)}, pred[1,8192]{1,0:T(4,128)(4,1)S(1)}, /*index=5*/f32[8192]{0:T(1024)S(...) while((s32[]{:T(128)}, f32[16]{0:T(128)S(1)}, ...), condition=%wide.region_7.8_spmd.clone, body=%wide.region_5.7_spmd.clone.sunk | while | flops 786563 | bytes 91005 | solution.py:35
  210.5 1.3 dynamic-slice
  212.8 23.5 %all-reduce = f32[256]{0:T(256)S(1)} all-reduce(f32[256]{0:T(256)S(1)} %fusion.40), channel_id=1, replica_groups=mesh['row'=16,'col'=32] {'row'}, use_global_device_ids=true, to_apply=%add | all-reduce | flops 256 | bytes 2048
  236.5 10.4 %while.35 = (s32[]{:T(128)}, f32[16,8192]{1,0:T(8,128)S(1)}, s32[16,16]{1,0:T(8,128)S(1)}, s32[8192]{0:T(1024)S(1)}, s32[16,16]{1,0:T(8,128)S(1)}, /*index=5*/f3...) while((s32[]{:T(128)}, f32[16,8192]{1,0:T(8,128)S(1)}, ...), condition=%wide.region_10.11_spmd, body=%wide.region_8.10_spmd.sunk | while | flops 1441810 | bytes 181013 | solution.py:137
  247.7 0.7 all-gather.4.cloned.1.call-update
  248.4 23.0 %gather_fusion = s32[4096]{0:T(1024)S(1)} fusion(s32[8192]{0:T(1024)S(1)} %get-tuple-element.539, s32[4096]{0:T(1024)S(1)} %get-tuple-element.264), kind=kCustom, calls=%fused_computation | custom fusion | bytes 49152 | tf_op jit(solution)/shard_map/gather | solution.py:75
  271.5 23.0 %gather_fusion.3 = f32[4096]{0:T(1024)S(1)} fusion(f32[8192]{0:T(1024)S(1)} %get-tuple-element.538, s32[4096]{0:T(1024)S(1)} %get-tuple-element.264), kind=kCustom, calls=%fused_computation.3 | custom fusion | bytes 49152 | tf_op jit(solution)/shard_map/gather | solution.py:73
  294.6 32.0 %all-gather.6.cloned.1.call-done = f32[262144]{0:T(1024)} async-done(((f32[8192]{0:T(1024)}), f32[262144]{0:T(1024)}) %all-gather.6.cloned.1.call-update) | async-done | bytes 1048592 | tf_op jit(solution)/shard_map/all_gather | solution.py:138
  326.6 1.4 reshape.167
  328.1 23.0 %gather_fusion.2 = f32[4096]{0:T(1024)S(1)} fusion(f32[8192]{0:T(1024)S(1)} %get-tuple-element.267, s32[4096]{0:T(1024)S(1)} %get-tuple-element.264), kind=kCustom, calls=%fused_computation.2 | custom fusion | bytes 49152 | tf_op jit(solution)/shard_map/gather | solution.py:74
  351.2 8.1 %while.36 = (s32[]{:T(128)}, f32[16,16]{1,0:T(8,128)S(1)}, s32[16,16]{1,0:T(8,128)S(1)}, s32[8192]{0:T(1024)S(1)}, f32[1,8192]{1,0:T(1,128)S(1)}, /*index=5*/f32...) while((s32[]{:T(128)}, f32[16,16]{1,0:T(8,128)S(1)}, ...), condition=%wide.region_15.16_spmd, body=%wide.region_13.15_spmd.sunk | while | flops 925714 | bytes 115569 | solution.py:144
  359.3 77.3 %all-gather.4.cloned.1.call-done = f32[512,4096]{1,0:T(8,128)} async-done(((f32[512,128]{1,0:T(8,128)}), f32[512,4096]{1,0:T(8,128)}) %all-gather.4.cloned.1.call-update) | async-done | bytes 8388624 | tf_op jit(solution)/shard_map/all_gather | solution.py:147
  436.6 19.3 %fusion.34 = f32[512,256]{0,1:T(8,128)S(1)} fusion(f32[512,4096]{1,0:T(8,128)} %all-gather.4.cloned.1.call-done, s32[256]{0:T(256)S(1)} %iota_add_fusion, f32[256]{0:T(256)S(1)} %div.58, f32[256]{0:T(256)S(1)} %all-reduce, f32[256]{0:T(256)S(1)} %dynamic_slice.52, f32[4096]{0:T(1024)S(1)} %gather_fusion.3, f32[4096]{0:T(1024)S(1)} %gather_fusion.2, ...), kind=kOutput, calls=%fused_computation.60 | convolution fusion | flops 6452936704 | bytes 8970496 | tf_op jit(solution)/shard_map/dot_general | solution.py:160
  455.9 1.0 copy.9
  (375 shorter events, 64.7 us)
Async XLA Ops:
  6.5 110.8 %copy-start = (f32[8192]{0:T(1024)S(1)}, f32[8192]{0:T(1024)}, u32[]{:S(2)}) copy-start(f32[8192]{0:T(1024)} %param.12) | copy-start | bytes 98308
  6.5 320.0 %all-gather.6.cloned.1.call-start = ((), (), s32[]{:S(2)}) async-start(), calls=%async_computation.1 | async-start | bytes 1081344 | tf_op jit(solution)/shard_map/all_gather | solution.py:138
  117.3 95.2 %copy-start.1 = (s32[8192]{0:T(1024)S(1)}, s32[8192]{0:T(1024)}, u32[]{:S(2)}) copy-start(s32[8192]{0:T(1024)} %param.13) | copy-start | bytes 98308
  117.3 131.1 %copy-start.2 = (s32[8192]{0:T(1024)S(1)}, s32[8192]{0:T(1024)}, u32[]{:S(2)}) copy-start(s32[8192]{0:T(1024)} %param.14) | copy-start | bytes 98308
  247.6 189.0 %all-gather.4.cloned.1.call-start = ((), (), s32[]{:S(2)}) async-start(), calls=%async_computation | async-start | bytes 8650752 | tf_op jit(solution)/shard_map/all_gather | solution.py:147
Sparse Core Ops, SparseCore 0:
  247.7 78.7 all-gather.5
  329.6 106.9 all-gather.3
